TPU v7x, 128 devices: a whole 4x4x4 slice. The times are simulated.
128 devices in a mesh: tok: 4 (over y), vocab: 32 (over x, z, core).
Axes of the slice: x: 4, y: 4, z: 4, core: 2. Of those that a mesh axis runs over, the one named last changes fastest.
Arguments:
- teacher_logits: bfloat16 [512, 131072], P('tok', 'vocab'), may hold values from -18 to 240
- hidden: bfloat16 [512, 4608], P('tok'), may hold values from -6 to 6
- new_head: bfloat16 [4608, 131072], P(None, ('tok', 'vocab')), may hold values from -0.26516504 to 0.26516504
- labels: int32 [512], replicated, may hold values from 0 to 131071
- map_target: int32 [1024, 4], P('vocab'), may hold values from 0 to 1023, as said below
- map_weight: bfloat16 [1024, 4, 128, 128], P('vocab'), may hold values from 0 to 0.017578125, as said below
Outputs:
- loss: float32 [512], P('tok')
- head_grad: bfloat16 [4608, 131072], P(None, ('tok', 'vocab'))
Inputs may be any that keep to these rules, and one draw needn't show every extreme that they name: `map_target`: values are ids of new blocks; new block b belongs to the device at index b // 8 of tok and vocab together, tok first. Of the 128 entries of one vocab index, at most 2 belong to one device, and some device gets exactly 2. `map_weight`: entries are non-negative.
All inputs are finite; a program needn't handle non-finite values.
Results may differ from a plain program's by a relative error of at most 0.001.
The roundings to bfloat16 on the way count: a program that leaves them out, or rounds other values in their place, can miss the bound.
Values may be sent and summed in bfloat16 or wider, within the bound.
A program may use at most 128 MiB of HBM per device.

v0:
```python
import jax
import jax.numpy as jnp
from jax import lax
from jax.sharding import PartitionSpec as P


def local(teacher_logits, hidden, new_head, labels, map_target, map_weight):
    tok_rows = teacher_logits.shape[0]
    block = map_weight.shape[2]
    fanout = map_weight.shape[1]
    old_blocks = map_target.shape[0]
    entries = old_blocks * fanout
    n_tok = lax.axis_size("tok")
    n_vocab = lax.axis_size("vocab")
    nodes = n_tok * n_vocab
    capacity = max(2, 2 * entries // nodes)
    new_cols = new_head.shape[1]
    per_node = new_cols // block
    own_index = lax.axis_index(("tok", "vocab"))
    scores = teacher_logits.astype(jnp.float32)
    local_top = jnp.max(scores, axis=1)
    highest = lax.pmax(local_top, "vocab")
    total = lax.psum(jnp.sum(jnp.exp(scores - highest[:, None]), axis=1), "vocab")
    teacher_prob = (jnp.exp(scores - highest[:, None]) / total[:, None]).astype(jnp.bfloat16)
    pieces = teacher_prob.reshape(tok_rows, old_blocks, block)
    contrib = jnp.einsum("tjb,jkbc->jktc", pieces, map_weight, preferred_element_type=jnp.float32)
    contrib = contrib.astype(jnp.bfloat16).reshape(entries, tok_rows, block)
    owners = (map_target // per_node).reshape(entries)
    earlier = jnp.arange(entries)[None, :] < jnp.arange(entries)[:, None]
    slots = jnp.sum((owners[:, None] == owners[None, :]) & earlier, axis=1)
    outbox = (
        jnp.zeros((nodes, capacity, tok_rows, block), jnp.bfloat16).at[owners, slots].set(contrib)
    )
    inbox = lax.all_to_all(outbox, ("tok", "vocab"), split_axis=0, concat_axis=0, tiled=True)
    inbox = inbox.reshape(n_tok, n_vocab, capacity, tok_rows, block)
    targets_all = lax.all_gather(map_target, "vocab", axis=0, tiled=True).reshape(n_vocab, entries)
    owners_all = targets_all // per_node
    local_block = targets_all % per_node
    slots_all = jnp.sum((owners_all[:, :, None] == owners_all[:, None, :]) & earlier[None], axis=2)
    picked = (owners_all == own_index)[:, :, None] & (
        slots_all[:, :, None] == jnp.arange(capacity)[None, None, :]
    )
    block_hit = local_block[:, :, None] == jnp.arange(per_node)[None, None, :]
    landing = jnp.einsum(
        "vec,veb->vcb", picked.astype(jnp.float32), block_hit.astype(jnp.float32)
    ).astype(jnp.bfloat16)
    target = jnp.einsum("vcb,svctk->stbk", landing, inbox, preferred_element_type=jnp.float32)
    target = target.reshape(n_tok * tok_rows, new_cols)
    everyone = lax.all_gather(hidden, "tok", axis=0, tiled=True)
    logits = jnp.dot(everyone, new_head, preferred_element_type=jnp.float32)
    columns = own_index * new_cols + jnp.arange(new_cols, dtype=jnp.int32)
    label_hit = labels[:, None] == columns[None, :]
    label_part = jnp.sum(jnp.where(label_hit, logits, 0.0), axis=1)
    mass_part = jnp.sum(target, axis=1)
    inner_part = jnp.sum(target * logits, axis=1)
    row_top = jnp.max(logits, axis=1)
    top_all = lax.pmax(row_top, ("tok", "vocab"))
    exp_part = jnp.sum(jnp.exp(logits - top_all[:, None]), axis=1)
    total_all, target_mass, inner, label_logit = lax.psum(
        (exp_part, mass_part, inner_part, label_part), ("tok", "vocab")
    )
    log_total = top_all + jnp.log(total_all)
    loss_all = target_mass * log_total - inner + log_total - label_logit
    loss = lax.dynamic_slice_in_dim(loss_all, lax.axis_index("tok") * tok_rows, tok_rows)
    probs = jnp.exp(logits - log_total[:, None])
    grad_logits = (
        (target_mass + 1.0)[:, None] * probs - target - label_hit.astype(jnp.float32)
    ).astype(jnp.bfloat16)
    head_grad = lax.dot_general(
        everyone, grad_logits, (((0,), (0,)), ((), ())), preferred_element_type=jnp.float32
    )
    return (loss, head_grad.astype(jnp.bfloat16))


def solution(mesh):
    return jax.shard_map(
        local,
        mesh=mesh,
        in_specs=(
            P("tok", "vocab"),
            P("tok", None),
            P(None, ("tok", "vocab")),
            P(),
            P("vocab", None),
            P("vocab", None, None, None),
        ),
        out_specs=(P("tok"), P(None, ("tok", "vocab"))),
        check_vma=False,
    )
```

profile of v0, /device:TPU:1, one launch (start us, length us, event | category | flops | bytes accessed | tf_op | source)
XLA Modules:
  0.0 477.8 jit_solution(10782458382185194525)
XLA Ops:
  7.2 0.0 all-gather.3.cloned.1.call-start
  7.2 0.7 all-gather.3.cloned.1.call-update
  7.9 0.7 add_select_fusion.2
  8.6 0.1 copy.44
  8.7 0.1 eq.79
  8.8 0.1 reshape.176
  8.9 1.5 reduce_max.23
  10.4 64.8 %pmax.14 = f32[128]{0:T(128)S(1)} all-reduce(bf16[128]{0:T(256)(128)(2,1)S(1)} %reduce_max.23), channel_id=1, replica_groups=mesh['tok'=4,'vocab'=32] {'vocab'}, use_global_device_ids=true, to_apply=%region_2.0 | all-reduce | flops 128 | bytes 768 | tf_op jit(solution)/shard_map/pmax | solution.py:22
  75.2 0.5 fusion.7
  75.7 67.0 %psum.35 = f32[128]{0:T(128)S(1)} all-reduce(f32[128]{0:T(128)S(1)} %fusion.7), channel_id=1, replica_groups=mesh['tok'=4,'vocab'=32] {'vocab'}, use_global_device_ids=true, to_apply=%region_4.5 | all-reduce | flops 128 | bytes 1024 | tf_op jit(solution)/shard_map/psum | solution.py:23
  142.7 0.5 fusion.9
  143.2 0.2 copy.62
  143.5 0.2 convert_reduce_fusion.1
  143.6 1.3 copy-done.2
  144.9 3.2 convolution_convert_fusion.1
  148.1 5.5 %broadcast_in_dim.5 = bf16[128,2,128,128]{3,2,1,0:T(8,128)(2,1)} broadcast(bf16[]{:T(256)} %constant.50.clone.1), dimensions={} | broadcast | bytes 8388610 | tf_op jit(solution)/shard_map/broadcast_in_dim | solution.py:32
  153.6 20.7 %scatter_fusion = bf16[128,2,128,128]{3,2,1,0:T(8,128)(2,1)} fusion(bf16[128,2,128,128]{3,2,1,0:T(8,128)(2,1)} %broadcast_in_dim.5, s32[128]{0:T(128)S(1)} %fusion.26, bf16[128,128,128]{2,1,0:T(8,128)(2,1)} %bitcast.43), kind=kCustom, calls=%fused_computation | custom fusion | bytes 12583936 | tf_op jit(solution)/shard_map/scatter | solution.py:32
  174.4 5.4 %all-to-all-start = ((bf16[128,2,128,128]{3,2,1,0:T(8,128)(2,1)}), bf16[128,2,128,128]{3,2,1,0:T(8,128)(2,1)}, u32[]{:S(2)}, u32[]{:S(2)}) async-start(bf16[128,2,128,128]{3,2,1,0:T(8,128)(2,1)} %scatter_fusion), calls=%async_computation | async-start | bytes 16777216 | tf_op jit(solution)/shard_map/all_to_all | solution.py:34
  179.8 117.2 %all-gather = s32[32,32,4]{1,2,0:T(4,128)S(1)} all-gather(s32[1,32,4]{1,2,0:T(4,128)S(1)} %bitcast.47), channel_id=1, replica_groups=mesh['tok'=4,'vocab'=32] {'vocab'}, dimensions={0}, use_global_device_ids=true | all-gather | bytes 16896 | tf_op jit(solution)/shard_map/all_gather | solution.py:36
  297.0 0.1 copy.47
  297.1 0.1 copy.48
  297.2 1.3 convert_reduce_fusion
  298.5 0.2 fusion.8
  298.7 0.0 all-gather.3.cloned.1.call-done
  298.7 10.1 %fusion.27 = (f32[512]{0:T(512)S(1)}, f32[512,1024]{1,0:T(8,128)}) fusion(bf16[512,4608]{1,0:T(8,128)(2,1)} %all-gather.3.cloned.1.call-done, bf16[4608,1024]{1,0:T(8,128)(2,1)} %param.8), kind=kOutput, calls=%fused_computation.64 | convolution fusion | flops 4832361984 | bytes 16254976 | tf_op jit(solution)/shard_map/dot_general | solution.py:50
  308.8 65.0 %pmax.15 = f32[512]{0:T(512)S(1)} all-reduce(f32[512]{0:T(512)S(1)} %get-tuple-element.24), channel_id=1, replica_groups=mesh['tok'=4,'vocab'=32] {'tok','vocab'}, use_global_device_ids=true, to_apply=%region_10.11 | all-reduce | flops 512 | bytes 4096 | tf_op jit(solution)/shard_map/pmax | solution.py:57
  373.9 8.9 %bitcast_reduce_fusion = (f32[4,128]{1,0:T(4,128)S(1)}, f32[4,128,128,8,1]{2,3,4,1,0:T(8,128)S(1)}) fusion(bf16[32,2,8,1,1]{2,1,0,4,3:T(2,128)(2,1)S(1)} %fusion.8, bf16[4,32,2,128,128]{4,3,2,1,0:T(8,128)(2,1)} %bitcast.5), kind=kOutput, calls=%fused_computation.14 | convolution fusion | flops 67632640 | bytes 10488832 | tf_op jit(solution)/shard_map/vcb,svctk->stbk/dot_general | solution.py:47
  382.8 1.2 fusion.6
  384.0 62.9 %all-reduce = (f32[512]{0:T(512)S(1)}, f32[512]{0:T(512)S(1)}, f32[512]{0:T(512)S(1)}, f32[512]{0:T(512)S(1)}) all-reduce(f32[512]{0:T(512)S(1)} %get-tuple-element.13, f32[512]{0:T(512)S(1)} %get-tuple-element.14, f32[512]{0:T(512)S(1)} %get-tuple-element.12, f32[512]{0:T(512)S(1)} %bitcast.46), channel_id=1, replica_groups=mesh['tok'=4,'vocab'=32] {'tok','vocab'}, use_global_device_ids=true, to_apply=%region_16.17 | all-reduce | flops 2048 | bytes 16384 | tf_op jit(solution)/shard_map/psum | solution.py:59
  446.8 10.9 %fusion.2 = bf16[4608,1024]{0,1:T(8,128)(2,1)} fusion(bf16[512,4608]{1,0:T(8,128)(2,1)} %all-gather.3.cloned.1.call-done, f32[512,1024]{1,0:T(8,128)} %get-tuple-element.25, f32[64,8,8,128]{3,2,1,0:T(8,128)S(1)} %bitcast.42, f32[512]{0:T(512)S(1)} %get-tuple-element.20, f32[512]{0:T(512)S(1)} %get-tuple-element.23, s32[1024]{0:T(1024)S(1)} %iota_add_fusion, ...), kind=kOutput, calls=%fused_computation.4 | convolution fusion | flops 4840226816 | bytes 18360320 | tf_op jit(solution)/shard_map/dot_general | solution.py:69
  457.8 12.6 %copy.54 = bf16[4608,1024]{1,0:T(8,128)(2,1)} copy(bf16[4608,1024]{0,1:T(8,128)(2,1)} %fusion.2) | data formatting | bytes 18874368
  470.4 0.6 dynamic_slice.3
  (16 shorter events, 0.1 us)
Async XLA Ops:
  7.2 68.0 %copy-start = (bf16[128,4096]{1,0:T(8,128)(2,1)S(1)}, bf16[128,4096]{1,0:T(8,128)(2,1)}, u32[]{:S(2)}) copy-start(bf16[128,4096]{1,0:T(8,128)(2,1)} %param.6) | copy-start | bytes 3145732
  7.2 291.5 %all-gather.3.cloned.1.call-start = ((), (), s32[]{:S(2)}) async-start(), calls=%async_computation.1 | async-start | bytes 5898240 | tf_op jit(solution)/shard_map/all_gather | solution.py:49
  142.7 2.2 copy-start.2
  174.4 5.4 %copy-start.4 = (s32[32,4]{0,1:T(4,128)S(1)}, s32[32,4]{0,1:T(4,128)}, u32[]{:S(2)}) copy-start(s32[32,4]{0,1:T(4,128)} %param.10) | copy-start | bytes 1540
  174.4 199.5 %all-to-all-start = ((bf16[128,2,128,128]{3,2,1,0:T(8,128)(2,1)}), bf16[128,2,128,128]{3,2,1,0:T(8,128)(2,1)}, u32[]{:S(2)}, u32[]{:S(2)}) async-start(bf16[128,2,128,128]{3,2,1,0:T(8,128)(2,1)} %scatter_fusion), calls=%async_computation | async-start | bytes 16777216 | tf_op jit(solution)/shard_map/all_to_all | solution.py:34
  373.8 8.9 %copy-start.1 = (f32[512,1024]{1,0:T(8,128)S(1)}, f32[512,1024]{1,0:T(8,128)}, u32[]{:S(2)}) copy-start(f32[512,1024]{1,0:T(8,128)} %get-tuple-element.25) | copy-start | bytes 6291460
  373.9 8.9 %copy-start.3 = (s32[512]{0:T(512)S(1)}, s32[512]{0:T(512)}, u32[]{:S(2)}) copy-start(s32[512]{0:T(512)} %param.9) | copy-start | bytes 6148
Sparse Core Ops, SparseCore 0:
  9.7 55.8 all-gather.2
where the time goes:
time: 479 us; the launch traced here: 478 us
  blocking collectives  377 us (79%)
  local copies, waits for them, and re-layouts  41.4 us (9%)
  matrix products  33.3 us (7%)
  between operations  14.2 us (3%)
  other arithmetic  5.87 us (1%)
  starting transfers between devices  5.46 us (1%)
    all_gather x1, blocking collectives, local(): lax.all_gather(map_target, 'vocab', axis=0, tiled=True)  117 us
    psum x1, blocking collectives, local(): lax.psum(jnp.sum(jnp.exp(scores - highest[:, None]), axis=1), 'vocab')  67 us
    pmax x1, blocking collectives, local(): top_all = lax.pmax(row_top, ('tok', 'vocab'))  65 us
    pmax x1, blocking collectives, local(): highest = lax.pmax(local_top, 'vocab')  64.8 us
    psum x1, blocking collectives, local(): lax.psum((exp_part, mass_part, inner_part, label_part), ('tok', 'vocab'))  62.9 us
    scatter x1, local copies, waits for them, and re-layouts, local(): jnp.zeros((nodes, capacity, tok_rows, block), jnp.bfloat16)  20.7 us
    unnamed x12, local copies, waits for them, and re-layouts  14.1 us
    dot_general x1, matrix products, local(): lax.dot_general(everyone, grad_logits, (((0,), (0,)), ((), ())), preferre...  10.9 us
  transfers between devices with their start and end apart: 2, of which 0 were waited for; matrix products, arithmetic and copies ran while one was open for 9% of the time, Pallas kernels for 0%

commit v1 on v0

--- a/solution.py
+++ b/solution.py
@@ -33,7 +33,9 @@
     )
     inbox = lax.all_to_all(outbox, ("tok", "vocab"), split_axis=0, concat_axis=0, tiled=True)
     inbox = inbox.reshape(n_tok, n_vocab, capacity, tok_rows, block)
-    targets_all = lax.all_gather(map_target, "vocab", axis=0, tiled=True).reshape(n_vocab, entries)
+    targets_all = jnp.concatenate(
+        lax.all_to_all(jnp.stack([map_target] * lax.axis_size("vocab")), "vocab", 0, 0), axis=0
+    ).reshape(n_vocab, entries)
     owners_all = targets_all // per_node
     local_block = targets_all % per_node
     slots_all = jnp.sum((owners_all[:, :, None] == owners_all[:, None, :]) & earlier[None], axis=2)

time: 479 us -> 452 us (0.944)
  blocking collectives: 377 us -> 339 us
  starting transfers between devices: 5.46 us -> 14.8 us
    all_gather x1 -> x0, blocking collectives: 117 us -> none  [local(): lax.all_gather(map_target, 'vocab', axis=0, tiled=True)]
    pmax x1, blocking collectives: 65 us -> 144 us  [local(): top_all = lax.pmax(row_top, ('tok', 'vocab'))]
    all_to_all x0 -> x1, starting transfers between devices: none -> 9.43 us  [local(): lax.all_to_all(jnp.stack([map_target] * lax.axis_size('vocab')), 'vocab',...]
    unnamed x12 -> x13, local copies, waits for them, and re-layouts: 14.1 us -> 15.7 us
  transfers between devices with their start and end apart: 2 -> 3, of which waited for: 0 -> 0; matrix products, arithmetic and copies ran while one was open for 9% -> 10% of each run, Pallas kernels for 0% -> 0%
where the time goes in v1:
time: 452 us; the launch traced here: 451 us
  blocking collectives  339 us (75%)
  local copies, waits for them, and re-layouts  43.5 us (10%)
  matrix products  33.3 us (7%)
  starting transfers between devices  14.8 us (3%)
  between operations  14.2 us (3%)
  other arithmetic  5.33 us (1%)
    pmax x1, blocking collectives, local(): top_all = lax.pmax(row_top, ('tok', 'vocab'))  144 us
    psum x1, blocking collectives, local(): lax.psum(jnp.sum(jnp.exp(scores - highest[:, None]), axis=1), 'vocab')  67.4 us
    psum x1, blocking collectives, local(): lax.psum((exp_part, mass_part, inner_part, label_part), ('tok', 'vocab'))  64.8 us
    pmax x1, blocking collectives, local(): highest = lax.pmax(local_top, 'vocab')  62.5 us
    scatter x1, local copies, waits for them, and re-layouts, local(): jnp.zeros((nodes, capacity, tok_rows, block), jnp.bfloat16)  20.7 us
    unnamed x13, local copies, waits for them, and re-layouts  15.7 us
    dot_general x1, matrix products, local(): lax.dot_general(everyone, grad_logits, (((0,), (0,)), ((), ())), preferre...  11 us
    dot_general x1, matrix products, local(): logits = jnp.dot(everyone, new_head, preferred_element_type=jnp.float32)  10.1 us
  transfers between devices with their start and end apart: 3, of which 0 were waited for; matrix products, arithmetic and copies ran while one was open for 10% of the time, Pallas kernels for 0%

profile of v1, /device:TPU:1, one launch (start us, length us, event | category | flops | bytes accessed | tf_op | source)
XLA Modules:
  0.0 450.8 jit_solution(8474738600645579342)
XLA Ops:
  7.2 0.8 broadcast_bitcast_fusion
  8.0 0.7 reshape.189
  8.7 9.4 %all-to-all-start.1 = ((s32[32,1,128]{2,1,0:T(1,128)}), s32[32,1,128]{2,1,0:T(1,128)S(1)}, u32[]{:S(2)}, u32[]{:S(2)}) async-start(s32[32,1,128]{2,1,0:T(1,128)} %reshape.189), calls=%async_computation.1 | async-start | bytes 32768 | tf_op jit(solution)/shard_map/all_to_all | solution.py:37
  18.1 0.7 all-gather.2.cloned.1.call-update
  18.8 0.7 add_select_fusion.2
  19.6 0.1 eq.79
  19.7 0.1 reshape.175
  19.8 0.2 reduce_max.23
  20.1 62.5 %pmax.14 = f32[128]{0:T(128)S(1)} all-reduce(bf16[128]{0:T(256)(128)(2,1)S(1)} %reduce_max.23), channel_id=1, replica_groups=mesh['tok'=4,'vocab'=32] {'vocab'}, use_global_device_ids=true, to_apply=%region_2.0 | all-reduce | flops 128 | bytes 768 | tf_op jit(solution)/shard_map/pmax | solution.py:22
  82.6 0.5 fusion.7
  83.1 67.4 %psum.35 = f32[128]{0:T(128)S(1)} all-reduce(f32[128]{0:T(128)S(1)} %fusion.7), channel_id=1, replica_groups=mesh['tok'=4,'vocab'=32] {'vocab'}, use_global_device_ids=true, to_apply=%region_4.5 | all-reduce | flops 128 | bytes 1024 | tf_op jit(solution)/shard_map/psum | solution.py:23
  150.4 0.5 fusion.9
  150.9 0.2 copy.75
  151.2 0.2 convert_reduce_fusion.1
  151.4 1.3 copy-done.2
  152.6 3.2 convolution_convert_fusion.1
  155.8 5.5 %broadcast_in_dim.5 = bf16[128,2,128,128]{3,2,1,0:T(8,128)(2,1)} broadcast(bf16[]{:T(256)} %constant.50.clone.1), dimensions={} | broadcast | bytes 8388610 | tf_op jit(solution)/shard_map/broadcast_in_dim | solution.py:32
  161.4 20.7 %scatter_fusion = bf16[128,2,128,128]{3,2,1,0:T(8,128)(2,1)} fusion(bf16[128,2,128,128]{3,2,1,0:T(8,128)(2,1)} %broadcast_in_dim.5, s32[128]{0:T(128)S(1)} %fusion.26, bf16[128,128,128]{2,1,0:T(8,128)(2,1)} %bitcast.45), kind=kCustom, calls=%fused_computation | custom fusion | bytes 12583936 | tf_op jit(solution)/shard_map/scatter | solution.py:32
  182.1 5.3 %all-to-all-start = ((bf16[128,2,128,128]{3,2,1,0:T(8,128)(2,1)}), bf16[128,2,128,128]{3,2,1,0:T(8,128)(2,1)}, u32[]{:S(2)}, u32[]{:S(2)}) async-start(bf16[128,2,128,128]{3,2,1,0:T(8,128)(2,1)} %scatter_fusion), calls=%async_computation | async-start | bytes 16777216 | tf_op jit(solution)/shard_map/all_to_all | solution.py:34
  187.4 0.5 broadcast.187
  187.9 0.7 reduce.2
  188.7 0.1 copy.60
  188.9 1.3 convert_reduce_fusion
  190.3 0.2 fusion.8
  190.5 10.1 %fusion.27 = (f32[512]{0:T(512)S(1)}, f32[512,1024]{1,0:T(8,128)}) fusion(bf16[512,4608]{1,0:T(8,128)(2,1)} %all-gather.2.cloned.1.call-done, bf16[4608,1024]{1,0:T(8,128)(2,1)} %param.8), kind=kOutput, calls=%fused_computation.64 | convolution fusion | flops 4832361984 | bytes 16254976 | tf_op jit(solution)/shard_map/dot_general | solution.py:52
  200.5 144.3 %pmax.15 = f32[512]{0:T(512)S(1)} all-reduce(f32[512]{0:T(512)S(1)} %get-tuple-element.26), channel_id=1, replica_groups=mesh['tok'=4,'vocab'=32] {'tok','vocab'}, use_global_device_ids=true, to_apply=%region_10.11 | all-reduce | flops 512 | bytes 4096 | tf_op jit(solution)/shard_map/pmax | solution.py:59
  344.9 8.9 %bitcast_reduce_fusion = (f32[4,128]{1,0:T(4,128)S(1)}, f32[4,128,128,8,1]{2,3,4,1,0:T(8,128)S(1)}) fusion(bf16[32,2,8,1,1]{2,1,0,4,3:T(2,128)(2,1)S(1)} %fusion.8, bf16[4,32,2,128,128]{4,3,2,1,0:T(8,128)(2,1)} %bitcast.5), kind=kOutput, calls=%fused_computation.14 | convolution fusion | flops 67632640 | bytes 10488832 | tf_op jit(solution)/shard_map/vcb,svctk->stbk/dot_general | solution.py:49
  353.8 1.2 fusion.6
  355.0 64.8 %all-reduce = (f32[512]{0:T(512)S(1)}, f32[512]{0:T(512)S(1)}, f32[512]{0:T(512)S(1)}, f32[512]{0:T(512)S(1)}) all-reduce(f32[512]{0:T(512)S(1)} %get-tuple-element.15, f32[512]{0:T(512)S(1)} %get-tuple-element.16, f32[512]{0:T(512)S(1)} %get-tuple-element.14, f32[512]{0:T(512)S(1)} %bitcast.49), channel_id=1, replica_groups=mesh['tok'=4,'vocab'=32] {'tok','vocab'}, use_global_device_ids=true, to_apply=%region_16.17 | all-reduce | flops 2048 | bytes 16384 | tf_op jit(solution)/shard_map/psum | solution.py:61
  419.8 11.0 %fusion.2 = bf16[4608,1024]{0,1:T(8,128)(2,1)} fusion(bf16[512,4608]{1,0:T(8,128)(2,1)} %all-gather.2.cloned.1.call-done, f32[512,1024]{1,0:T(8,128)} %get-tuple-element.27, f32[64,8,8,128]{3,2,1,0:T(8,128)S(1)} %bitcast.44, f32[512]{0:T(512)S(1)} %get-tuple-element.22, f32[512]{0:T(512)S(1)} %get-tuple-element.25, s32[1024]{0:T(1024)S(1)} %iota_add_fusion, ...), kind=kOutput, calls=%fused_computation.4 | convolution fusion | flops 4840226816 | bytes 18360320 | tf_op jit(solution)/shard_map/dot_general | solution.py:71
  430.8 12.6 %copy.67 = bf16[4608,1024]{1,0:T(8,128)(2,1)} copy(bf16[4608,1024]{0,1:T(8,128)(2,1)} %fusion.2) | data formatting | bytes 18874368
  443.4 0.6 dynamic_slice.3
  (20 shorter events, 0.4 us)
Async XLA Ops:
  7.2 12.7 %copy-start = (bf16[128,4096]{1,0:T(8,128)(2,1)S(1)}, bf16[128,4096]{1,0:T(8,128)(2,1)}, u32[]{:S(2)}) copy-start(bf16[128,4096]{1,0:T(8,128)(2,1)} %param.6) | copy-start | bytes 3145732
  8.7 173.4 %all-to-all-start.1 = ((s32[32,1,128]{2,1,0:T(1,128)}), s32[32,1,128]{2,1,0:T(1,128)S(1)}, u32[]{:S(2)}, u32[]{:S(2)}) async-start(s32[32,1,128]{2,1,0:T(1,128)} %reshape.189), calls=%async_computation.1 | async-start | bytes 32768 | tf_op jit(solution)/shard_map/all_to_all | solution.py:37
  18.1 172.3 %all-gather.2.cloned.1.call-start = ((), (), s32[]{:S(2)}) async-start(), calls=%async_computation.2 | async-start | bytes 5898240 | tf_op jit(solution)/shard_map/all_gather | solution.py:51
  150.4 2.2 copy-start.2
  182.1 162.8 %all-to-all-start = ((bf16[128,2,128,128]{3,2,1,0:T(8,128)(2,1)}), bf16[128,2,128,128]{3,2,1,0:T(8,128)(2,1)}, u32[]{:S(2)}, u32[]{:S(2)}) async-start(bf16[128,2,128,128]{3,2,1,0:T(8,128)(2,1)} %scatter_fusion), calls=%async_computation | async-start | bytes 16777216 | tf_op jit(solution)/shard_map/all_to_all | solution.py:34
  344.9 8.9 %copy-start.1 = (f32[512,1024]{1,0:T(8,128)S(1)}, f32[512,1024]{1,0:T(8,128)}, u32[]{:S(2)}) copy-start(f32[512,1024]{1,0:T(8,128)} %get-tuple-element.27) | copy-start | bytes 6291460
  344.9 8.9 %copy-start.3 = (s32[512]{0:T(512)S(1)}, s32[512]{0:T(512)}, u32[]{:S(2)}) copy-start(s32[512]{0:T(512)} %param.9) | copy-start | bytes 6148
Sparse Core Ops, SparseCore 0:
  20.6 53.7 all-gather.1
